TPU v7x, 32 devices: a whole 2x2x4 slice. The times are simulated.
32 devices in a mesh: groups: 2 (over y), blk: 4 (over z), uly: 4 (over x, core).
Axes of the slice: x: 2, y: 2, z: 4, core: 2. Of those that a mesh axis runs over, the one named last changes fastest.
Arguments:
- queries: bfloat16 [2048, 32, 128], P(('groups', 'blk', 'uly')), parts along dimension 0, may hold values from -160 to 160
- key_states: bfloat16 [2048, 32, 128], P(('groups', 'blk', 'uly')), parts along dimension 0, may hold values from -4 to 4
- value_states: bfloat16 [2048, 32, 128], P(('groups', 'blk', 'uly')), parts along dimension 0, may hold values from -6 to 6
- block_list: int32 [16, 8], P('groups'), parts along dimension 0, may hold values from -1 to 7, as said below
- valid_count: int32 [2], P('groups'), parts along dimension 0, may hold values from 897 to 1024
Outputs:
- attended: bfloat16 [2048, 32, 128], P(('groups', 'blk', 'uly')), parts along dimension 0
There are 2 independent parts, one for each index of `groups`. A program takes and returns all parts, laid end to end along the dimension named above; each array names one. Nothing has to cross between parts.
Inputs may be any that keep to these rules, and one draw needn't show every extreme that they name: `block_list`: row i lists, in ascending order, the key blocks that query block i may attend, each once, and the rest of the row is -1; block 0 and block i are always listed.
All inputs are finite; a program needn't handle non-finite values.
Results may differ from a plain program's by a relative error of at most 0.0055.
Values may be sent and summed in bfloat16 or wider, within the bound.
A program may use at most 64 MiB of HBM per device.

v0:
```python
import math

import jax
import jax.numpy as jnp
from jax import lax
from jax.sharding import PartitionSpec as P

BLOCK = 128


def from_behind(value, axis, steps):
    count = lax.axis_size(axis)
    pairs = [(source, (source + steps) % count) for source in range(count)]
    return lax.ppermute(value, axis, pairs)


def local(queries, key_states, value_states, block_list, valid_count):
    blk_count = lax.axis_size("blk")
    uly_count = lax.axis_size("uly")
    my_place = lax.axis_index("blk")
    entry_rows = queries.shape[0]
    head_count = queries.shape[1]
    head_size = queries.shape[2]
    local_heads = head_count // uly_count
    row_count = entry_rows * uly_count
    own_queries, own_keys, own_values = (
        lax.all_to_all(queries, "uly", split_axis=1, concat_axis=0, tiled=True),
        lax.all_to_all(key_states, "uly", split_axis=1, concat_axis=0, tiled=True),
        lax.all_to_all(value_states, "uly", split_axis=1, concat_axis=0, tiled=True),
    )

    def token_places(owner):
        return owner * row_count + jnp.arange(row_count, dtype=jnp.int32)

    block_total = block_list.shape[0]
    allowed = jnp.any(
        block_list[:, :, None] == jnp.arange(block_total, dtype=jnp.int32)[None, None, :], axis=1
    )
    query_mask = jnp.take(allowed, token_places(my_place) // BLOCK, axis=0)
    limit = valid_count[0]
    factor = 1.0 / math.sqrt(head_size)

    def accumulate(state, key_value, live):
        highest, totals, summed = state
        scores = (
            jnp.einsum(
                "qhd,khd->hqk", own_queries, key_value[0], preferred_element_type=jnp.float32
            )
            * factor
        )
        masked = jnp.where(live[None], scores, -1e30)
        new_high = jnp.maximum(highest, jnp.max(masked, axis=-1))
        rescale = jnp.exp(highest - new_high)
        weights = jnp.where(live[None], jnp.exp(masked - new_high[:, :, None]), 0.0)
        totals = totals * rescale + jnp.sum(weights, axis=-1)
        summed = summed * rescale[:, :, None] + jnp.einsum(
            "hqk,khd->hqd",
            weights.astype(jnp.bfloat16),
            key_value[1],
            preferred_element_type=jnp.float32,
        )
        return (new_high, totals, summed)

    def attend(state, key_value, owner):
        key_spots = token_places(owner)
        live = jnp.take(query_mask, key_spots // BLOCK, axis=1) & (key_spots < limit)[None, :]
        return accumulate(state, key_value, live)

    start_state = (
        jnp.full((local_heads, row_count), -1e30, jnp.float32),
        jnp.zeros((local_heads, row_count), jnp.float32),
        jnp.zeros((local_heads, row_count, head_size), jnp.float32),
    )
    held = jnp.stack([own_keys, own_values])
    state = attend(start_state, held, my_place)

    def visit(hop_index, carried):
        travelling, inner = carried
        travelling = from_behind(travelling, "blk", 1)
        owner = (my_place - hop_index) % blk_count
        return (travelling, attend(inner, travelling, owner))

    _, (highest, totals, summed) = lax.fori_loop(1, blk_count, visit, (held, state))
    result = (summed / totals[:, :, None]).astype(jnp.bfloat16)
    result = jnp.transpose(result, (1, 0, 2))
    return lax.all_to_all(result, "uly", split_axis=0, concat_axis=1, tiled=True)


def solution(mesh):
    placed = (
        P(("groups", "blk", "uly"), None, None),
        P(("groups", "blk", "uly"), None, None),
        P(("groups", "blk", "uly"), None, None),
        P("groups", None),
        P("groups"),
    )
    return jax.shard_map(
        local,
        mesh=mesh,
        in_specs=placed,
        out_specs=P(("groups", "blk", "uly"), None, None),
        check_vma=False,
    )
```

profile of v0, /device:TPU:0, one launch (start us, length us, event | category | flops | bytes accessed | tf_op | source)
XLA Modules:
  0.0 146.5 jit_solution(18166487798598785277)
XLA Ops:
  0.0 2.1 %copy.41 = bf16[64,32,128]{2,0,1:T(8,128)(2,1)} copy(bf16[64,32,128]{2,1,0:T(8,128)(2,1)} %param.9) | data formatting | bytes 1048576 | tf_op args[0]
  2.1 4.2 %all-to-all-start.2 = ((bf16[64,32,128]{2,0,1:T(8,128)(2,1)}), bf16[64,32,128]{2,0,1:T(8,128)(2,1)S(1)}, u32[]{:S(2)}, u32[]{:S(2)}) async-start(bf16[64,32,128]{2,0,1:T(8,128)(2,1)} %copy.41), calls=%async_computation.2 | async-start | bytes 1048576 | tf_op jit(solution)/shard_map/all_to_all | solution.py:27
  7.1 1.0 copy.36
  8.1 0.8 gather_fusion.1
  9.1 6.1 %all-to-all-done.2 = bf16[64,32,128]{2,0,1:T(8,128)(2,1)S(1)} async-done(((bf16[64,32,128]{2,0,1:T(8,128)(2,1)}), bf16[64,32,128]{2,0,1:T(8,128)(2,1)S(1)}, u32[]{:S(2)}, u32[]{:S(2)}) %all-to-all-start.2) | async-done | bytes 524320 | tf_op jit(solution)/shard_map/all_to_all | solution.py:27
  15.2 3.5 %all-to-all-start = ((bf16[64,32,128]{2,0,1:T(8,128)(2,1)}), bf16[64,32,128]{2,0,1:T(8,128)(2,1)S(1)}, u32[]{:S(2)}, u32[]{:S(2)}) async-start(bf16[64,32,128]{2,0,1:T(8,128)(2,1)} %copy.36), calls=%async_computation | async-start | bytes 1048576 | tf_op jit(solution)/shard_map/all_to_all | solution.py:28
  18.8 1.0 copy.38
  19.8 1.1 gather_fusion.2
  20.8 0.1 bitcast_and_fusion.1
  21.0 6.5 %all-to-all-done = bf16[64,32,128]{2,0,1:T(8,128)(2,1)S(1)} async-done(((bf16[64,32,128]{2,0,1:T(8,128)(2,1)}), bf16[64,32,128]{2,0,1:T(8,128)(2,1)S(1)}, u32[]{:S(2)}, u32[]{:S(2)}) %all-to-all-start) | async-done | bytes 524320 | tf_op jit(solution)/shard_map/all_to_all | solution.py:28
  27.5 4.1 %all-to-all-start.1 = ((bf16[64,32,128]{2,0,1:T(8,128)(2,1)}), bf16[64,32,128]{2,0,1:T(8,128)(2,1)}, u32[]{:S(2)}, u32[]{:S(2)}) async-start(bf16[64,32,128]{2,0,1:T(8,128)(2,1)} %copy.38), calls=%async_computation.1 | async-start | bytes 1048576 | tf_op jit(solution)/shard_map/all_to_all | solution.py:29
  31.7 0.5 fusion.14
  32.2 0.5 fusion.16
  32.7 7.8 %all-to-all-done.1 = bf16[64,32,128]{2,0,1:T(8,128)(2,1)} async-done(((bf16[64,32,128]{2,0,1:T(8,128)(2,1)}), bf16[64,32,128]{2,0,1:T(8,128)(2,1)}, u32[]{:S(2)}, u32[]{:S(2)}) %all-to-all-start.1) | async-done | bytes 524320 | tf_op jit(solution)/shard_map/all_to_all | solution.py:29
  40.5 1.1 copy.39
  41.6 2.0 %convolution_add_fusion.1 = f32[8,256,128]{2,1,0:T(8,128)} fusion(bf16[256,8,128]{2,0,1:T(8,128)(2,1)S(1)} %bitcast.58, f32[8,256,256]{1,2,0:T(8,128)S(1)} %get-tuple-element.295, f32[8,256]{1,0:T(8,128)S(1)} %broadcast_maximum_fusion, pred[256,256]{0,1:T(8,128)(4,1)S(1)} %bitcast_and_fusion.1, f32[8,256]{1,0:T(8,128)S(1)} %get-tuple-element.292), kind=kOutput, calls=%fused_computation.37 | convolution fusion | flops 137101312 | bytes 3751936 | tf_op jit(solution)/shard_map/hqk,khd->hqd/dot_general | solution.py:56
  43.6 1.1 pad_maximum_fusion
  44.7 0.5 copy-done
  45.2 88.3 %while.21 = (s32[]{:T(128)}, bf16[2,256,8,128]{3,1,2,0:T(8,128)(2,1)}, f32[8,256]{1,0:T(8,128)S(1)}, f32[8,256]{1,0:T(8,128)S(1)}, f32[8,256,128]{2,1,0:T(8,128)...) while((s32[]{:T(128)}, ...), condition=%wide.region_6.8_spmd, body=%wide.region_3.7_spmd.sunk | while | flops 275922432 | bytes 16851260 | solution.py:83
  45.2 2.3 %collective-permute-start = (bf16[2,256,8,128]{3,1,2,0:T(8,128)(2,1)}, bf16[2,256,8,128]{3,1,2,0:T(8,128)(2,1)S(1)}, u32[]{:S(2)}, u32[]{:S(2)}) collective-permute-start(bf16[2,256,8,128]{3,1,2,0:T(8,128)(2,1)} %get-tuple-element.380), channel_id=1, source_target_pairs={{0,4},{4,8},{8,12},{12,0},{1,5},{5,9},{9,13},{13,1},{2,6},{6,10},{... | collective-permute-start | bytes 3145736 | tf_op jit(solution)/shard_map/while/body/eval_jaxpr/ppermute | solution.py:14
  47.5 1.1 gather_fusion
  48.6 0.7 compare_and_fusion.3
  49.2 0.1 bitcast_and_fusion.3
  49.4 23.3 %collective-permute-done = bf16[2,256,8,128]{3,1,2,0:T(8,128)(2,1)S(1)} collective-permute-done((bf16[2,256,8,128]{3,1,2,0:T(8,128)(2,1)}, bf16[2,256,8,128]{3,1,2,0:T(8,128)(2,1)S(1)}, u32[]{:S(2)}, u32[]{:S(2)}) %collective-permute-start) | collective-permute-done | bytes 1048608 | tf_op jit(solution)/shard_map/while/body/eval_jaxpr/ppermute | solution.py:14
  72.7 0.5 fusion.41
  73.2 0.5 fusion.42
  73.7 1.0 copy.68
  74.7 1.1 convolution_add_fusion.3
  75.9 1.1 gather_fusion
  77.0 0.7 compare_and_fusion.3
  77.7 0.1 bitcast_and_fusion.3
  77.8 24.2 %collective-permute-done = bf16[2,256,8,128]{3,1,2,0:T(8,128)(2,1)S(1)} collective-permute-done((bf16[2,256,8,128]{3,1,2,0:T(8,128)(2,1)}, bf16[2,256,8,128]{3,1,2,0:T(8,128)(2,1)S(1)}, u32[]{:S(2)}, u32[]{:S(2)}) %collective-permute-start) | collective-permute-done | bytes 1048608 | tf_op jit(solution)/shard_map/while/body/eval_jaxpr/ppermute | solution.py:14
  102.0 0.5 fusion.41
  102.5 0.5 fusion.42
  103.0 1.0 copy.68
  104.0 1.1 convolution_add_fusion.3
  105.3 1.1 gather_fusion
  106.3 0.7 compare_and_fusion.3
  107.0 0.1 bitcast_and_fusion.3
  107.1 23.3 %collective-permute-done = bf16[2,256,8,128]{3,1,2,0:T(8,128)(2,1)S(1)} collective-permute-done((bf16[2,256,8,128]{3,1,2,0:T(8,128)(2,1)}, bf16[2,256,8,128]{3,1,2,0:T(8,128)(2,1)S(1)}, u32[]{:S(2)}, u32[]{:S(2)}) %collective-permute-start) | collective-permute-done | bytes 1048608 | tf_op jit(solution)/shard_map/while/body/eval_jaxpr/ppermute | solution.py:14
  130.4 0.5 fusion.41
  130.9 0.5 fusion.42
  131.4 1.0 copy.68
  132.4 1.1 convolution_add_fusion.3
  133.5 0.1 copy.45
  133.7 0.7 fusion.24
  134.4 11.2 %all_to_all.72 = bf16[256,8,128]{2,1,0:T(8,128)(2,1)S(1)} all-to-all(bf16[256,8,128]{2,1,0:T(8,128)(2,1)S(1)} %fusion.24), channel_id=1, replica_groups=mesh['groups'=2,'blk'=4,'uly'=4] {'uly'}, dimensions={0} | all-to-all | bytes 1048576 | tf_op jit(solution)/shard_map/all_to_all | solution.py:86
  145.6 0.9 copy.56
  (36 shorter events, 0.6 us)
Async XLA Ops:
  0.0 6.4 %copy-start.3 = (s32[8,8]{1,0:T(8,128)S(1)}, s32[8,8]{1,0:T(8,128)}, u32[]{:S(2)}) copy-start(s32[8,8]{1,0:T(8,128)} %param.12) | copy-start | bytes 772
  0.0 7.1 %copy-start.1 = (bf16[64,32,128]{2,1,0:T(8,128)(2,1)S(1)}, bf16[64,32,128]{2,1,0:T(8,128)(2,1)}, u32[]{:S(2)}) copy-start(bf16[64,32,128]{2,1,0:T(8,128)(2,1)} %param.10) | copy-start | bytes 1572868
  0.0 18.8 %copy-start.2 = (bf16[64,32,128]{2,1,0:T(8,128)(2,1)S(1)}, bf16[64,32,128]{2,1,0:T(8,128)(2,1)}, u32[]{:S(2)}) copy-start(bf16[64,32,128]{2,1,0:T(8,128)(2,1)} %param.11) | copy-start | bytes 1572868
  2.1 13.1 %all-to-all-start.2 = ((bf16[64,32,128]{2,0,1:T(8,128)(2,1)}), bf16[64,32,128]{2,0,1:T(8,128)(2,1)S(1)}, u32[]{:S(2)}, u32[]{:S(2)}) async-start(bf16[64,32,128]{2,0,1:T(8,128)(2,1)} %copy.41), calls=%async_computation.2 | async-start | bytes 1048576 | tf_op jit(solution)/shard_map/all_to_all | solution.py:27
  15.2 12.3 %all-to-all-start = ((bf16[64,32,128]{2,0,1:T(8,128)(2,1)}), bf16[64,32,128]{2,0,1:T(8,128)(2,1)S(1)}, u32[]{:S(2)}, u32[]{:S(2)}) async-start(bf16[64,32,128]{2,0,1:T(8,128)(2,1)} %copy.36), calls=%async_computation | async-start | bytes 1048576 | tf_op jit(solution)/shard_map/all_to_all | solution.py:28
  27.5 13.0 %all-to-all-start.1 = ((bf16[64,32,128]{2,0,1:T(8,128)(2,1)}), bf16[64,32,128]{2,0,1:T(8,128)(2,1)}, u32[]{:S(2)}, u32[]{:S(2)}) async-start(bf16[64,32,128]{2,0,1:T(8,128)(2,1)} %copy.38), calls=%async_computation.1 | async-start | bytes 1048576 | tf_op jit(solution)/shard_map/all_to_all | solution.py:29
  43.6 1.6 %copy-start = (f32[8,256,128]{2,1,0:T(8,128)S(1)}, f32[8,256,128]{2,1,0:T(8,128)}, u32[]{:S(2)}) copy-start(f32[8,256,128]{2,1,0:T(8,128)} %convolution_add_fusion.1) | copy-start | bytes 3145732
  45.2 27.5 %collective-permute-start = (bf16[2,256,8,128]{3,1,2,0:T(8,128)(2,1)}, bf16[2,256,8,128]{3,1,2,0:T(8,128)(2,1)S(1)}, u32[]{:S(2)}, u32[]{:S(2)}) collective-permute-start(bf16[2,256,8,128]{3,1,2,0:T(8,128)(2,1)} %get-tuple-element.380), channel_id=1, source_target_pairs={{0,4},{4,8},{8,12},{12,0},{1,5},{5,9},{9,13},{13,1},{2,6},{6,10},{... | collective-permute-start | bytes 3145736 | tf_op jit(solution)/shard_map/while/body/eval_jaxpr/ppermute | solution.py:14
  75.8 26.2 %collective-permute-start = (bf16[2,256,8,128]{3,1,2,0:T(8,128)(2,1)}, bf16[2,256,8,128]{3,1,2,0:T(8,128)(2,1)S(1)}, u32[]{:S(2)}, u32[]{:S(2)}) collective-permute-start(bf16[2,256,8,128]{3,1,2,0:T(8,128)(2,1)} %get-tuple-element.380), channel_id=1, source_target_pairs={{0,4},{4,8},{8,12},{12,0},{1,5},{5,9},{9,13},{13,1},{2,6},{6,10},{... | collective-permute-start | bytes 3145736 | tf_op jit(solution)/shard_map/while/body/eval_jaxpr/ppermute | solution.py:14
  105.1 25.3 %collective-permute-start = (bf16[2,256,8,128]{3,1,2,0:T(8,128)(2,1)}, bf16[2,256,8,128]{3,1,2,0:T(8,128)(2,1)S(1)}, u32[]{:S(2)}, u32[]{:S(2)}) collective-permute-start(bf16[2,256,8,128]{3,1,2,0:T(8,128)(2,1)} %get-tuple-element.380), channel_id=1, source_target_pairs={{0,4},{4,8},{8,12},{12,0},{1,5},{5,9},{9,13},{13,1},{2,6},{6,10},{... | collective-permute-start | bytes 3145736 | tf_op jit(solution)/shard_map/while/body/eval_jaxpr/ppermute | solution.py:14
where the time goes:
time: 147 us
  waiting for transfers between devices  91.2 us (62%)
  local copies, waits for them, and re-layouts  14.9 us (10%)
  starting transfers between devices  14.2 us (10%)
  blocking collectives  11.2 us (8%)
  matrix products  7.24 us (5%)
  other arithmetic  6.72 us (5%)
    ppermute x3, waiting for transfers between devices, from_behind(): return lax.ppermute(value, axis, pairs)  70.8 us
    all_to_all x1, blocking collectives, local(): lax.all_to_all(result, 'uly', split_axis=0, concat_axis=1, tiled=True)  11.2 us
    all_to_all x1, waiting for transfers between devices, local(): lax.all_to_all(value_states, 'uly', split_axis=1, concat_axis=0, tiled=True)  7.83 us
    all_to_all x1, waiting for transfers between devices, local(): lax.all_to_all(key_states, 'uly', split_axis=1, concat_axis=0, tiled=True)  6.46 us
    all_to_all x1, waiting for transfers between devices, local(): lax.all_to_all(queries, 'uly', split_axis=1, concat_axis=0, tiled=True)  6.12 us
    dot_general x4, matrix products, accumulate(): jnp.einsum('hqk,khd->hqd', weights.astype(jnp.bfloat16), key_value[1], pr...  5.36 us
    unnamed x11, local copies, waits for them, and re-layouts  4.69 us
    gather x4, local copies, waits for them, and re-layouts, attend(): jnp.take(query_mask, key_spots // BLOCK, axis=1)  4.22 us
  transfers between devices with their start and end apart: 6, of which 6 were waited for; matrix products, arithmetic and copies ran while one was open for 8% of the time, Pallas kernels for 0%

commit v1 on v0

--- a/solution.py
+++ b/solution.py
@@ -1,8 +1,11 @@
+import functools
 import math
 
 import jax
 import jax.numpy as jnp
 from jax import lax
+from jax.experimental import pallas as pl
+from jax.experimental.pallas import tpu as pltpu
 from jax.sharding import PartitionSpec as P
 
 BLOCK = 128
@@ -86,7 +89,280 @@
     return lax.all_to_all(result, "uly", split_axis=0, concat_axis=1, tiled=True)
 
 
+MESH = pl.DeviceIdType.MESH
+DEAD = -1e30
+
+
+def exchange_kernel(
+    chips,
+    uly_count,
+    heads,
+    rows,
+    q_in,
+    k_in,
+    v_in,
+    list_ref,
+    count_ref,
+    out_ref,
+    q_buf,
+    k_buf,
+    v_buf,
+    o_buf,
+    bias_ref,
+    in_send,
+    in_recv,
+    out_send,
+    out_recv,
+    own_sem,
+    own_out_sem,
+):
+    me = lax.axis_index("blk") * uly_count + lax.axis_index("uly")
+    my_chip = me // 2
+    my_core = me % 2
+    sibling = my_chip * 2 + 1 - my_core
+    sources = (k_in, v_in, q_in)
+    buffers = (k_buf, v_buf, q_buf)
+    seq = chips * 2 * rows
+
+    def place(device):
+        return {"blk": device // uly_count, "uly": device % uly_count}
+
+    def partner(step):
+        chip = 0
+        bit = 1
+        while bit < chips:
+            chip = chip + ((my_chip // bit + step // bit) % 2) * bit
+            bit *= 2
+        return chip
+
+    def token_rows(device):
+        return pl.ds(pl.multiple_of(device * rows, rows), rows)
+
+    def in_copy(kind, head, step, device, dest_core):
+        return pltpu.make_async_remote_copy(
+            src_ref=sources[kind].at[device * heads + head],
+            dst_ref=buffers[kind].at[head, token_rows(me)],
+            send_sem=in_send.at[kind, head, step, dest_core],
+            recv_sem=in_recv.at[kind, head, step, my_core],
+            device_id=place(device),
+            device_id_type=MESH,
+        )
+
+    def in_wait(kind, head, step, device, source_core):
+        pltpu.make_async_remote_copy(
+            src_ref=sources[kind].at[device * heads + head],
+            dst_ref=buffers[kind].at[head, token_rows(device)],
+            send_sem=in_send.at[kind, head, step, source_core],
+            recv_sem=in_recv.at[kind, head, step, source_core],
+            device_id=place(device),
+            device_id_type=MESH,
+        ).wait_recv()
+
+    def own_copy(kind, head):
+        return pltpu.make_async_copy(
+            sources[kind].at[me * heads + head],
+            buffers[kind].at[head, token_rows(me)],
+            own_sem.at[kind, head],
+        )
+
+    def out_copy(head, step, device, dest_core):
+        return pltpu.make_async_remote_copy(
+            src_ref=o_buf.at[head, token_rows(device)],
+            dst_ref=out_ref.at[me * heads + head],
+            send_sem=out_send.at[head, step, dest_core],
+            recv_sem=out_recv.at[head, step, my_core],
+            device_id=place(device),
+            device_id_type=MESH,
+        )
+
+    def out_wait(head, step, device, source_core):
+        pltpu.make_async_remote_copy(
+            src_ref=o_buf.at[head, token_rows(device)],
+            dst_ref=out_ref.at[device * heads + head],
+            send_sem=out_send.at[head, step, source_core],
+            recv_sem=out_recv.at[head, step, source_core],
+            device_id=place(device),
+            device_id_type=MESH,
+        ).wait_recv()
+
+    def own_out(head):
+        return pltpu.make_async_copy(
+            o_buf.at[head, token_rows(me)], out_ref.at[me * heads + head], own_out_sem.at[head]
+        )
+
+    def each_partner(body):
+        def visit(index, carried):
+            step = chips - 1 - index
+            chip = partner(step)
+            for core in range(2):
+                body(step, chip * 2 + core, core)
+            return carried
+
+        lax.fori_loop(0, chips - 1, visit, 0)
+
+    barrier = pltpu.get_barrier_semaphore()
+
+    def greet(step, device, core):
+        pl.semaphore_signal(barrier, inc=1, device_id=place(device), device_id_type=MESH)
+
+    each_partner(greet)
+    pl.semaphore_signal(barrier, inc=1, device_id=place(sibling), device_id_type=MESH)
+    for head in range(heads):
+        for kind in range(3):
+            own_copy(kind, head).start()
+    pl.semaphore_wait(barrier, chips * 2 - 1)
+
+    for head in range(heads):
+        for kind in range(3):
+            each_partner(
+                lambda step, device, core: in_copy(kind, head, step, device, core).start()
+            )
+            in_copy(kind, head, 0, sibling, 0).start()
+
+    block_total = list_ref.shape[0]
+    spots = lax.broadcasted_iota(jnp.int32, (block_total, seq), 1)
+    owners = spots // BLOCK
+    listed = list_ref[...]
+    live = owners == listed[:, 0:1]
+    for column in range(1, block_total):
+        live = live | (owners == listed[:, column : column + 1])
+    live = live & (spots < count_ref[0])
+    bias_ref[...] = jnp.where(live, 0.0, DEAD)
+    factor = (1.0 / math.sqrt(q_buf.shape[2])) * math.log2(math.e)
+    chip_rows = 2 * rows
+
+    def attend(head, chip):
+        span = pl.ds(pl.multiple_of(chip * chip_rows, chip_rows), chip_rows)
+        scores = lax.dot_general(
+            q_buf[head, span, :],
+            k_buf[head],
+            (((1,), (1,)), ((), ())),
+            preferred_element_type=jnp.float32,
+        )
+        bias = bias_ref[pl.ds(chip * chip_rows // BLOCK, 1), :]
+        masked = scores * factor + bias
+        highest = jnp.max(masked, axis=-1, keepdims=True)
+        weights = jnp.exp2(masked - highest)
+        totals = jnp.sum(weights, axis=-1, keepdims=True)
+        mixed = jnp.dot(
+            weights.astype(jnp.bfloat16), v_buf[head], preferred_element_type=jnp.float32
+        )
+        o_buf[head, span, :] = (mixed / totals).astype(jnp.bfloat16)
+
+    def wait_sibling(kind, head):
+        pltpu.make_async_remote_copy(
+            src_ref=sources[kind].at[sibling * heads + head],
+            dst_ref=buffers[kind].at[head, token_rows(sibling)],
+            send_sem=in_send.at[kind, head, 0, 0],
+            recv_sem=in_recv.at[kind, head, 0, 1 - my_core],
+            device_id=place(sibling),
+            device_id_type=MESH,
+        ).wait_recv()
+
+    for head in range(heads):
+        for kind in range(2):
+            own_copy(kind, head).wait()
+            wait_sibling(kind, head)
+            each_partner(
+                lambda step, device, core: in_wait(kind, head, step, device, core)
+            )
+
+        def work(index, carried):
+            step = chips - 1 - index
+            chip = partner(step)
+            for core in range(2):
+                in_wait(2, head, step, chip * 2 + core, core)
+            attend(head, chip)
+            for core in range(2):
+                out_copy(head, step, chip * 2 + core, core).start()
+            return carried
+
+        lax.fori_loop(0, chips - 1, work, 0)
+        own_copy(2, head).wait()
+        wait_sibling(2, head)
+        attend(head, my_chip)
+        out_copy(head, 0, sibling, 0).start()
+        own_out(head).start()
+
+    for head in range(heads):
+        for kind in range(3):
+            each_partner(
+                lambda step, device, core: in_copy(kind, head, step, device, core).wait_send()
+            )
+            in_copy(kind, head, 0, sibling, 0).wait_send()
+        each_partner(
+            lambda step, device, core: out_copy(head, step, device, core).wait_send()
+        )
+        out_copy(head, 0, sibling, 0).wait_send()
+        each_partner(lambda step, device, core: out_wait(head, step, device, core))
+        pltpu.make_async_remote_copy(
+            src_ref=o_buf.at[head, token_rows(sibling)],
+            dst_ref=out_ref.at[sibling * heads + head],
+            send_sem=out_send.at[head, 0, 0],
+            recv_sem=out_recv.at[head, 0, 1 - my_core],
+            device_id=place(sibling),
+            device_id_type=MESH,
+        ).wait_recv()
+        own_out(head).wait()
+
+
+def whole_heads(blk_count, uly_count, queries, key_states, value_states, block_list, valid_count):
+    rows, head_count, head_size = queries.shape
+    devices = blk_count * uly_count
+    chips = devices // 2
+    heads = head_count // devices
+    seq = rows * devices
+
+    def by_head(value):
+        return jnp.transpose(value, (1, 0, 2))
+
+    result = pl.pallas_call(
+        functools.partial(exchange_kernel, chips, uly_count, heads, rows),
+        out_shape=jax.ShapeDtypeStruct((head_count, rows, head_size), jnp.bfloat16),
+        in_specs=[pl.BlockSpec(memory_space=pl.ANY)] * 3
+        + [
+            pl.BlockSpec(memory_space=pltpu.VMEM),
+            pl.BlockSpec(memory_space=pltpu.SMEM),
+        ],
+        out_specs=pl.BlockSpec(memory_space=pl.ANY),
+        scratch_shapes=[pltpu.VMEM((heads, seq, head_size), jnp.bfloat16)] * 4
+        + [
+            pltpu.VMEM((block_list.shape[0], seq), jnp.float32),
+            pltpu.SemaphoreType.DMA((3, heads, chips, 2)),
+            pltpu.SemaphoreType.DMA((3, heads, chips, 2)),
+            pltpu.SemaphoreType.DMA((heads, chips, 2)),
+            pltpu.SemaphoreType.DMA((heads, chips, 2)),
+            pltpu.SemaphoreType.DMA((3, heads)),
+            pltpu.SemaphoreType.DMA((heads,)),
+        ],
+        compiler_params=pltpu.CompilerParams(
+            collective_id=0, has_side_effects=True, vmem_limit_bytes=32 * 1024 * 1024
+        ),
+    )(by_head(queries), by_head(key_states), by_head(value_states), block_list, valid_count)
+    return jnp.transpose(result, (1, 0, 2))
+
+
+def fits_whole_heads(blk_count, uly_count, rows, head_count):
+    devices = blk_count * uly_count
+    return (
+        head_count % devices == 0
+        and devices >= 4
+        and devices & (devices - 1) == 0
+        and uly_count % 2 == 0
+        and BLOCK % (2 * rows) == 0
+        and rows % 16 == 0
+    )
+
+
 def solution(mesh):
+    blk_count, uly_count = mesh.shape["blk"], mesh.shape["uly"]
+
+    def step(queries, *rest):
+        rows, head_count, _ = queries.shape
+        if fits_whole_heads(blk_count, uly_count, rows, head_count):
+            return whole_heads(blk_count, uly_count, queries, *rest)
+        return local(queries, *rest)
+
     placed = (
         P(("groups", "blk", "uly"), None, None),
         P(("groups", "blk", "uly"), None, None),
@@ -95,7 +371,7 @@
         P("groups"),
     )
     return jax.shard_map(
-        local,
+        step,
         mesh=mesh,
         in_specs=placed,
         out_specs=P(("groups", "blk", "uly"), None, None),

time: 147 us -> 58.8 us (0.40)
  waiting for transfers between devices: 91.2 us -> 0 us
  Pallas kernels: 0 us -> 54.8 us
  starting transfers between devices: 14.2 us -> 0 us
  local copies, waits for them, and re-layouts: 14.9 us -> 3.15 us
  blocking collectives: 11.2 us -> 0 us
  matrix products: 7.24 us -> 0 us
  other arithmetic: 6.72 us -> 0 us
    ppermute x3 -> x0, waiting for transfers between devices: 70.8 us -> none  [from_behind(): return lax.ppermute(value, axis, pairs)]
    pallas_call x0 -> x1, Pallas kernels: none -> 54.8 us  [whole_heads(): pl.pallas_call(functools.partial(exchange_kernel, chips, uly_count, heads...]
    all_to_all x3 -> x0, waiting for transfers between devices: 20.4 us -> none  [the longest x1 7.83 us: local(): lax.all_to_all(value_states, 'uly', split_axis=1, concat_axis=0, tiled=True)]
    all_to_all x3 -> x0, starting transfers between devices: 11.8 us -> none  [the longest x1 4.21 us: local(): lax.all_to_all(queries, 'uly', split_axis=1, concat_axis=0, tiled=True)]
    all_to_all x1 -> x0, blocking collectives: 11.2 us -> none  [local(): lax.all_to_all(result, 'uly', split_axis=0, concat_axis=1, tiled=True)]
    dot_general x8 -> x0, matrix products: 7.24 us -> none  [the longest x4 5.36 us: accumulate(): jnp.einsum('hqk,khd->hqd', weights.astype(jnp.bfloat16), key_value[1], pr...]
    gather x5 -> x0, local copies, waits for them, and re-layouts: 5.03 us -> none  [the longest x4 4.22 us: attend(): jnp.take(query_mask, key_spots // BLOCK, axis=1)]
    unnamed x11 -> x7, local copies, waits for them, and re-layouts: 4.69 us -> 1.61 us
  transfers between devices with their start and end apart: 6 -> 0, of which waited for: 6 -> 0; matrix products, arithmetic and copies ran while one was open for 8% -> 0% of each run, Pallas kernels for 0% -> 0%
where the time goes in v1:
time: 58.8 us; the launch traced here: 58.6 us
  Pallas kernels  54.8 us (93%)
  local copies, waits for them, and re-layouts  3.15 us (5%)
  between operations  0.71 us (1%)
    pallas_call x1, Pallas kernels, whole_heads(): pl.pallas_call(functools.partial(exchange_kernel, chips, uly_count, heads...  54.8 us
    unnamed x7, local copies, waits for them, and re-layouts  1.61 us

profile of v1, /device:TPU:0, one launch (start us, length us, event | category | flops | bytes accessed | tf_op | source)
XLA Modules:
  0.0 58.6 jit_solution(2423181441738561674)
XLA Ops:
  0.7 0.0 copy-start.1
  0.7 0.0 copy-start.2
  0.7 1.3 %copy.13 = bf16[64,32,128]{2,0,1:T(8,128)(2,1)S(1)} copy(bf16[64,32,128]{2,1,0:T(8,128)(2,1)} %param.5) | data formatting | bytes 1048576 | tf_op args[0]
  2.0 0.0 copy-done.1
  2.0 0.0 copy-done.2
  2.0 0.0 copy-start
  2.0 0.4 copy_bitcast_fusion
  2.5 0.3 copy-done
  2.7 54.8 %shard_map.55 = bf16[32,64,128]{2,1,0:T(8,128)(2,1)S(1)} custom-call(bf16[32,64,128]{2,1,0:T(8,128)(2,1)S(1)} %bitcast.8, bf16[32,64,128]{2,1,0:T(8,128)(2,1)S(1)} %get-tuple-element.6.k_in, bf16[32,64,128]{2,1,0:T(8,128)(2,1)S(1)} %get-tuple-element.5.v_in, s32[8,8]{1,0:T(8,128)S(1)} %copy-done, s32[1]{0:T(128)S(6)} %copy.14.count_ref), custom_call_target="tpu_custom_call" | custom-call | tf_op jit(solution)/shard_map/pallas_call | solution.py:319
  57.5 1.1 %copy.9 = bf16[64,32,128]{2,1,0:T(8,128)(2,1)} copy(bf16[64,32,128]{2,0,1:T(8,128)(2,1)S(1)} %bitcast.9) | data formatting | bytes 1048576 | tf_op jit(solution)/shard_map/transpose | solution.py:342
Async XLA Ops:
  0.7 1.4 %copy-start.1 = (bf16[64,32,128]{2,1,0:T(8,128)(2,1)S(1)}, bf16[64,32,128]{2,1,0:T(8,128)(2,1)}, u32[]{:S(2)}) copy-start(bf16[64,32,128]{2,1,0:T(8,128)(2,1)} %param.7) | copy-start | bytes 1572868
  0.7 1.4 %copy-start.2 = (bf16[64,32,128]{2,1,0:T(8,128)(2,1)S(1)}, bf16[64,32,128]{2,1,0:T(8,128)(2,1)}, u32[]{:S(2)}) copy-start(bf16[64,32,128]{2,1,0:T(8,128)(2,1)} %param.6) | copy-start | bytes 1572868
  2.0 0.7 %copy-start = (s32[8,8]{1,0:T(8,128)S(1)}, s32[8,8]{1,0:T(8,128)}, u32[]{:S(2)}) copy-start(s32[8,8]{1,0:T(8,128)} %list_ref.1) | copy-start | bytes 772

commit v2 on v1

--- a/solution.py
+++ b/solution.py
@@ -98,12 +98,19 @@
     uly_count,
     heads,
     rows,
+    q_hbm,
+    k_hbm,
+    v_hbm,
+    list_hbm,
+    count_ref,
+    out_ref,
+    list_ref,
+    q_raw,
+    k_raw,
+    v_raw,
     q_in,
     k_in,
     v_in,
-    list_ref,
-    count_ref,
-    out_ref,
     q_buf,
     k_buf,
     v_buf,
@@ -115,6 +122,7 @@
     out_recv,
     own_sem,
     own_out_sem,
+    load_sem,
 ):
     me = lax.axis_index("blk") * uly_count + lax.axis_index("uly")
     my_chip = me // 2
@@ -192,7 +200,7 @@
 
     def each_partner(body):
         def visit(index, carried):
-            step = chips - 1 - index
+            step = 1 + index
             chip = partner(step)
             for core in range(2):
                 body(step, chip * 2 + core, core)
@@ -200,6 +208,23 @@
 
         lax.fori_loop(0, chips - 1, visit, 0)
 
+    loads = [
+        pltpu.make_async_copy(whole, raw, load_sem.at[kind])
+        for kind, (whole, raw) in enumerate(
+            ((k_hbm, k_raw), (v_hbm, v_raw), (q_hbm, q_raw), (list_hbm, list_ref))
+        )
+    ]
+    for load in loads:
+        load.start()
+
+    def by_head(kind):
+        loads[kind].wait()
+        raw = (k_raw, v_raw, q_raw)[kind]
+        for start in range(0, rows, 16):
+            sources[kind][:, start : start + 16, :] = jnp.transpose(
+                raw[start : start + 16], (1, 0, 2)
+            )
+
     barrier = pltpu.get_barrier_semaphore()
 
     def greet(step, device, core):
@@ -207,18 +232,19 @@
 
     each_partner(greet)
     pl.semaphore_signal(barrier, inc=1, device_id=place(sibling), device_id_type=MESH)
+    by_head(0)
+    pl.semaphore_wait(barrier, chips * 2 - 1)
     for head in range(heads):
         for kind in range(3):
+            if head == 0 and kind > 0:
+                by_head(kind)
             own_copy(kind, head).start()
-    pl.semaphore_wait(barrier, chips * 2 - 1)
-
-    for head in range(heads):
-        for kind in range(3):
             each_partner(
                 lambda step, device, core: in_copy(kind, head, step, device, core).start()
             )
             in_copy(kind, head, 0, sibling, 0).start()
 
+    loads[3].wait()
     block_total = list_ref.shape[0]
     spots = lax.broadcasted_iota(jnp.int32, (block_total, seq), 1)
     owners = spots // BLOCK
@@ -268,7 +294,7 @@
             )
 
         def work(index, carried):
-            step = chips - 1 - index
+            step = 1 + index
             chip = partner(step)
             for core in range(2):
                 in_wait(2, head, step, chip * 2 + core, core)
@@ -313,19 +339,19 @@
     heads = head_count // devices
     seq = rows * devices
 
-    def by_head(value):
-        return jnp.transpose(value, (1, 0, 2))
-
     result = pl.pallas_call(
         functools.partial(exchange_kernel, chips, uly_count, heads, rows),
         out_shape=jax.ShapeDtypeStruct((head_count, rows, head_size), jnp.bfloat16),
-        in_specs=[pl.BlockSpec(memory_space=pl.ANY)] * 3
+        in_specs=[pl.BlockSpec(memory_space=pltpu.HBM)] * 3
         + [
-            pl.BlockSpec(memory_space=pltpu.VMEM),
+            pl.BlockSpec(memory_space=pltpu.HBM),
             pl.BlockSpec(memory_space=pltpu.SMEM),
         ],
         out_specs=pl.BlockSpec(memory_space=pl.ANY),
-        scratch_shapes=[pltpu.VMEM((heads, seq, head_size), jnp.bfloat16)] * 4
+        scratch_shapes=[pltpu.VMEM(block_list.shape, jnp.int32)]
+        + [pltpu.VMEM((rows, head_count, head_size), jnp.bfloat16)] * 3
+        + [pltpu.VMEM((head_count, rows, head_size), jnp.bfloat16)] * 3
+        + [pltpu.VMEM((heads, seq, head_size), jnp.bfloat16)] * 4
         + [
             pltpu.VMEM((block_list.shape[0], seq), jnp.float32),
             pltpu.SemaphoreType.DMA((3, heads, chips, 2)),
@@ -334,11 +360,12 @@
             pltpu.SemaphoreType.DMA((heads, chips, 2)),
             pltpu.SemaphoreType.DMA((3, heads)),
             pltpu.SemaphoreType.DMA((heads,)),
+            pltpu.SemaphoreType.DMA((4,)),
         ],
         compiler_params=pltpu.CompilerParams(
-            collective_id=0, has_side_effects=True, vmem_limit_bytes=32 * 1024 * 1024
+            collective_id=0, has_side_effects=True, vmem_limit_bytes=54528 * 1024
         ),
-    )(by_head(queries), by_head(key_states), by_head(value_states), block_list, valid_count)
+    )(queries, key_states, value_states, block_list, valid_count)
     return jnp.transpose(result, (1, 0, 2))
 
 

time: 58.8 us -> 55.9 us (0.951)
  Pallas kernels: 54.8 us -> 53.3 us
  local copies, waits for them, and re-layouts: 3.15 us -> 1.82 us
    pallas_call x1, Pallas kernels: 54.8 us -> 53.3 us  [whole_heads(): pl.pallas_call(functools.partial(exchange_kernel, chips, uly_count, heads...]
    unnamed x7 -> x2, local copies, waits for them, and re-layouts: 1.61 us -> 0.68 us
where the time goes in v2:
time: 55.9 us; the launch traced here: 55.8 us
  Pallas kernels  53.3 us (95%)
  local copies, waits for them, and re-layouts  1.82 us (3%)
  between operations  0.67 us (1%)
    pallas_call x1, Pallas kernels, whole_heads(): pl.pallas_call(functools.partial(exchange_kernel, chips, uly_count, heads...  53.3 us
    transpose x1, local copies, waits for them, and re-layouts, whole_heads(): return jnp.transpose(result, (1, 0, 2))  1.14 us

profile of v2, /device:TPU:0, one launch (start us, length us, event | category | flops | bytes accessed | tf_op | source)
XLA Modules:
  0.0 55.8 jit_solution(2038072417958373367)
XLA Ops:
  0.7 0.0 copy-start
  0.7 0.7 %copy-done = s32[8,8]{1,0:T(8,128)S(1)} copy-done((s32[8,8]{1,0:T(8,128)S(1)}, s32[8,8]{1,0:T(8,128)}, u32[]{:S(2)}) %copy-start) | copy-done | bytes 280
  1.3 53.3 %shard_map.55 = bf16[32,64,128]{2,1,0:T(8,128)(2,1)S(1)} custom-call(bf16[64,32,128]{2,1,0:T(8,128)(2,1)} %q_hbm.1, bf16[64,32,128]{2,1,0:T(8,128)(2,1)} %k_hbm.1, bf16[64,32,128]{2,1,0:T(8,128)(2,1)} %v_hbm.1, s32[8,8]{1,0:T(8,128)S(1)} %copy-done, s32[1]{0:T(128)S(6)} %copy.7.count_ref), custom_call_target="tpu_custom_call" | custom-call | tf_op jit(solution)/shard_map/pallas_call | solution.py:342
  54.6 1.1 %copy.6 = bf16[64,32,128]{2,1,0:T(8,128)(2,1)} copy(bf16[64,32,128]{2,0,1:T(8,128)(2,1)S(1)} %bitcast.1) | data formatting | bytes 1048576 | tf_op jit(solution)/shard_map/transpose | solution.py:369
Async XLA Ops:
  0.7 0.7 %copy-start = (s32[8,8]{1,0:T(8,128)S(1)}, s32[8,8]{1,0:T(8,128)}, u32[]{:S(2)}) copy-start(s32[8,8]{1,0:T(8,128)} %list_hbm.1) | copy-start | bytes 772
